TPU v7x, 32 devices: a whole 2x2x4 slice. The times are simulated.
32 devices in a mesh: parts: 2 (over y), gx: 4 (over z), gy: 4 (over x, core).
Axes of the slice: x: 2, y: 2, z: 4, core: 2. Of those that a mesh axis runs over, the one named last changes fastest.
Arguments:
- base_cond: float32 [3, 4, 32, 512], P(None, None, 'gx', 'gy'), may hold values from 0.5 to 2
- base_mass: float32 [4, 32, 512], P(None, 'gx', 'gy'), may hold values from 0.05 to 0.5
- fine_residual: float32 [8, 32, 512], P('parts', 'gx', 'gy'), parts along dimension 0, may hold values from -6 to 6
- point_index: int32 [2], P('parts'), parts along dimension 0, may hold values from 0 to 1048575
- gen_vector: int32 [32], replicated, may hold values from 1 to 1048575
- z_offset: int32 [1], replicated, may hold values from 0 to 508
Outputs:
- coarse_stencil: float32 [27, 4, 16, 256], P(None, 'parts', 'gx', 'gy'), parts along dimension 1
- coarse_solution: float32 [4, 16, 256], P('parts', 'gx', 'gy'), parts along dimension 0
There are 2 independent parts, one for each index of `parts`. A program takes and returns all parts, laid end to end along the dimension named above; an argument that names none is the same for every part. Nothing has to cross between parts.
All inputs are finite; a program needn't handle non-finite values.
Results may differ from a plain program's by a relative error of at most 0.0003.
Values sent between devices are 32-bit elements; how exact they have to be, the bound alone decides.
A program may use at most 128 MiB of HBM per device.

v0:
```python
import functools
import itertools
import math

import jax
import jax.numpy as jnp
from jax import lax
from jax.experimental import pallas as pl
from jax.experimental.pallas import tpu as pltpu
from jax.sharding import PartitionSpec as P

MESH = pl.DeviceIdType.MESH
NZG = 512
QMCN = 1048576
SWEEPS = 4
OMEGA = 0.6
MODES = 32
HALO = 4
CLASSES = list(itertools.product((0, 1), repeat=3))
FIELDS = 5
AXIS_FIELD = (2, 0, 1)
DIRECTIONS = [(sx, sy) for sx in (-1, 0, 1) for sy in (-1, 0, 1) if (sx, sy) != (0, 0)]
ROWS = 24
LANES = 128
VMEM_GRANT = 60 * 1024 * 1024


def cos_turns(turns):
    rest = 0.25 - jnp.abs(turns - jnp.round(turns))
    angle = rest * (2.0 * math.pi)
    square = angle * angle
    series = 1.0 / 6227020800.0
    for term in (-1.0 / 39916800.0, 1.0 / 362880.0, -1.0 / 5040.0, 1.0 / 120.0, -1.0 / 6.0, 1.0):
        series = series * square + term
    return series * angle


def shift(value, axis, step):
    if axis == 2:
        return pltpu.roll(value, (-step) % LANES, 1)
    return pltpu.roll(value, (-step * (1, 2)[axis]) % ROWS, 0)


def lanes_of(value, index):
    return jnp.take_along_axis(value, index, axis=1, mode="promise_in_bounds")


def flip(cls, axis):
    return tuple(1 - p if a == axis else p for a, p in enumerate(cls))


def split_lanes(tile, index):
    return lanes_of(tile, index)


def field_roots(point_ref, gen_ref, zoff_ref, x_first, y_first, nx_total, ny_total):
    point = point_ref[0, 0]
    lane = lax.broadcasted_iota(jnp.int32, (1, 2 * MODES), 1)
    mode = jnp.where(lane < MODES, lane, lane - MODES)
    shifts = jnp.zeros((1, 2 * MODES), jnp.int32)
    for k in range(MODES):
        shifts = jnp.where(mode == k, (point * gen_ref[k]) & (QMCN - 1), shifts)
    modef = mode.astype(jnp.float32)
    amplitude = (shifts.astype(jnp.float32) / QMCN - 0.5) * (1.2 / (1.0 + 0.5 * modef))
    freq_z = modef - 5.0 * jnp.floor((modef + 0.5) * 0.2)
    freq_x = (1 + (mode & 3)).astype(jnp.float32)
    phase = modef * (0.7 / (2.0 * math.pi)) - jnp.where(lane < MODES, 0.0, 0.25)
    row = lax.broadcasted_iota(jnp.int32, (ROWS, 1), 0)
    z_row = (zoff_ref[0, 0] + 2 * (row & 1)).astype(jnp.float32) + 0.5
    x_row = (x_first + 2 * ((row >> 1) - HALO)).astype(jnp.float32) + 0.5
    left = []
    for pz, px in itertools.product((0, 1), repeat=2):
        turns = (z_row + pz) * (freq_z / (2.0 * NZG)) + (x_row + px) * (freq_x / (2.0 * nx_total))
        left.append(amplitude * cos_turns(turns + phase))
    left = jnp.concatenate(left, axis=0)
    mode_row = lax.broadcasted_iota(jnp.int32, (2 * MODES, 1), 0)
    freq_y = (1 + ((mode_row >> 2) & 3)).astype(jnp.float32)
    quarter = jnp.where(mode_row < MODES, 0.0, 0.25)
    place = lax.broadcasted_iota(jnp.int32, (1, LANES), 1)
    coarse = jnp.where(place < LANES // 2 + HALO, place, place - LANES)
    right = []
    for py in (0, 1):
        y_place = (y_first + 2 * coarse + py).astype(jnp.float32) + 0.5
        right.append(cos_turns(freq_y * (y_place / (2.0 * ny_total)) + quarter))
    right = jnp.concatenate(right, axis=1)
    logs = jnp.dot(left, right, precision=lax.Precision.HIGHEST, preferred_element_type=jnp.float32)
    roots = jnp.exp(0.5 * logs)
    out = {}
    for n, (pz, px) in enumerate(itertools.product((0, 1), repeat=2)):
        for py in (0, 1):
            out[pz, px, py] = roots[n * ROWS:(n + 1) * ROWS, py * LANES:(py + 1) * LANES]
    return out


def coefficients(base, roots, x_first, y_first, nx_total, ny_total):
    row = lax.broadcasted_iota(jnp.int32, (ROWS, LANES), 0)
    place = lax.broadcasted_iota(jnp.int32, (ROWS, LANES), 1)
    x_even = x_first + 2 * ((row >> 1) - HALO)
    half = LANES // 2
    y_even = y_first + 2 * jnp.where(place < half + HALO, place, place - LANES)
    inside = (x_even >= 0) & (x_even < nx_total) & (y_even >= 0) & (y_even < ny_total)
    inside = inside & ((place < half + HALO) | (place >= LANES - HALO))
    closed = (
        inside & ((row & 1) == 0),
        inside & (x_even + 2 < nx_total),
        inside & (y_even + 2 < ny_total),
    )
    cond, mass, residual = {}, {}, {}
    for cls in CLASSES:
        for axis in range(3):
            other = roots[flip(cls, axis)]
            if cls[axis]:
                other = shift(other, axis, 1)
            value = base(AXIS_FIELD[axis], cls) * roots[cls] * other
            cond[axis, cls] = jnp.where(closed[axis] if cls[axis] else inside, value, 0.0)
        mass[cls] = jnp.where(inside, base(3, cls) * (roots[cls] * roots[cls]), 1.0)
        residual[cls] = jnp.where(inside, base(4, cls), 0.0)
    return cond, mass, residual


def galerkin(cond, mass, residual):
    low = {}
    for cls in CLASSES:
        for axis in range(3):
            own = cond[axis, flip(cls, axis)]
            low[axis, cls] = own if cls[axis] else shift(own, axis, -1)

    weight = {((0, 0, 0), (0, 0, 0)): None}
    for cls in sorted(CLASSES, key=sum)[1:]:
        odd = [a for a in range(3) if cls[a]]
        total = mass[cls]
        for a in odd:
            total = total + (low[a, cls] + cond[a, cls])
        recip = 1.0 / total
        for corner in itertools.product(*[(0, 1) if p else (0,) for p in cls]):
            summed = None
            for a in odd:
                face = cond[a, cls] if corner[a] else low[a, cls]
                part = weight[flip(cls, a), tuple(0 if b == a else s for b, s in enumerate(corner))]
                if part is None:
                    term = face
                else:
                    term = face * (shift(part, a, 1) if corner[a] else part)
                summed = term if summed is None else summed + term
            weight[cls, corner] = recip * summed

    def wanted(offset):
        return offset >= (0, 0, 0)

    parts = {}

    def add(corner, offset, value):
        slot = parts.setdefault(offset, {})
        slot[corner] = slot[corner] + value if corner in slot else value

    for cls in sorted(CLASSES, key=sum)[:-1]:
        even = [a for a in range(3) if not cls[a]]
        pairs = None
        for a in even:
            pair = low[a, cls] + cond[a, cls]
            pairs = pair if pairs is None else pairs + pair
        if sum(cls) == 0:
            pairs = pairs + mass[cls]
        corners = list(itertools.product(*[(0, 1) if p else (0,) for p in cls]))
        applied = {}
        for corner in corners:
            own = weight[cls, corner]
            centre = pairs if own is None else pairs * own
            for a in even:
                up = flip(cls, a)
                high = tuple(1 if b == a else s for b, s in enumerate(corner))
                to_low = cond[a, up] * weight[up, corner]
                to_high = cond[a, up] * weight[up, high]
                centre = centre - shift(to_high, a, -1) - cond[a, cls] * weight[up, corner]
                below = tuple(-1 if b == a else s for b, s in enumerate(corner))
                applied[below] = -shift(to_low, a, -1)
                applied[high] = -(cond[a, cls] * weight[up, high])
            applied[corner] = centre
        for corner in corners:
            own = weight[cls, corner]
            for target, value in applied.items():
                offset = tuple(t - s for t, s in zip(target, corner))
                if wanted(offset):
                    add(corner, offset, value if own is None else own * value)

    def collect(slot):
        for axis in range(3):
            merged = {}
            for corner, value in slot.items():
                if corner[axis] == 0:
                    merged[corner] = merged[corner] + value if corner in merged else value
            for corner, value in slot.items():
                if corner[axis] == 1:
                    key = tuple(0 if b == axis else s for b, s in enumerate(corner))
                    moved = shift(value, axis, -1)
                    merged[key] = merged[key] + moved if key in merged else moved
            slot = merged
        return slot[0, 0, 0]

    stencil = {offset: collect(slot) for offset, slot in parts.items()}
    for offset in list(stencil):
        if offset != (0, 0, 0):
            value = stencil[offset]
            for axis, step in enumerate(offset):
                if step:
                    value = shift(value, axis, -step)
            stencil[tuple(-o for o in offset)] = value

    slot = {(0, 0, 0): residual[0, 0, 0]}
    for (cls, corner), own in weight.items():
        if own is not None:
            term = own * residual[cls]
            slot[corner] = slot[corner] + term if corner in slot else term
    return stencil, collect(slot)


def sweep_all(stencil, rhs):
    row = lax.broadcasted_iota(jnp.int32, (ROWS, LANES), 0)
    place = lax.broadcasted_iota(jnp.int32, (ROWS, LANES), 1)
    reach = HALO - 1
    valid = (row >= 2) & (row < ROWS - 2)
    valid = valid & ((place < LANES // 2 + reach) | (place >= LANES - reach))
    scale = jnp.where(valid, OMEGA / jnp.where(valid, stencil[0, 0, 0], 1.0), 0.0)
    values = rhs * scale
    for _ in range(SWEEPS - 1):
        rest = rhs
        for dz in (-1, 0, 1):
            in_z = shift(values, 0, dz) if dz else values
            for dx in (-1, 0, 1):
                in_x = shift(in_z, 1, dx) if dx else in_z
                for dy in (-1, 0, 1):
                    in_y = shift(in_x, 2, dy) if dy else in_x
                    rest = rest - stencil[dz, dx, dy] * in_y
        values = values + rest * scale
    return values


def place_of(counts, widths):
    gx, gy = lax.axis_index("gx"), lax.axis_index("gy")
    (nx_devices, ny_devices), (width_x, width_y) = counts, widths
    return gx * width_x, gy * width_y, nx_devices * width_x, ny_devices * width_y


def exchange(
    counts, widths, cond_hbm, mass_hbm, res_hbm, point_hbm, gen_hbm, zoff_hbm,
    own_hbm, side, strips, roots_hbm,
    cond_in, mass_in, res_in, point_ref, gen_ref, zoff_ref, own, strip, roots_out,
    in_sem, send_sem, recv_sem, out_sem,
):
    parts_at = lax.axis_index("parts")
    gx, gy = lax.axis_index("gx"), lax.axis_index("gy")
    nx_devices, ny_devices = counts

    def present(sx, sy):
        conditions = []
        if sx:
            conditions.append(gx > 0 if sx < 0 else gx < nx_devices - 1)
        if sy:
            conditions.append(gy > 0 if sy < 0 else gy < ny_devices - 1)
        return functools.reduce(jnp.logical_and, conditions)

    barrier = pltpu.get_barrier_semaphore()
    neighbours = 0
    for sx, sy in DIRECTIONS:
        there = present(sx, sy)
        neighbours = neighbours + there.astype(jnp.int32)

        @pl.when(there)
        def _():
            pl.semaphore_signal(
                barrier, inc=1, device_id=(parts_at, gx + sx, gy + sy), device_id_type=MESH
            )

    loads = [
        pltpu.make_async_copy(source, target, in_sem.at[n])
        for n, (source, target) in enumerate(
            (
                (cond_hbm, cond_in),
                (mass_hbm, mass_in),
                (res_hbm, res_in),
                (point_hbm, point_ref),
                (gen_hbm, gen_ref),
                (zoff_hbm, zoff_ref),
            )
        )
    ]
    for load in loads:
        load.start()
    for load in loads:
        load.wait()

    lane = lax.broadcasted_iota(jnp.int32, (8, LANES), 1)
    half = LANES // 2
    to_halves = jnp.where(lane < half, 2 * lane, 2 * lane - (LANES - 1))
    step = lane & 15
    to_strip = step + jnp.where(
        step < 4, half - 4, jnp.where(step < 8, LANES - 8, jnp.where(step < 12, -8, half - 12))
    )
    packs = [None] * 3
    for field in range(FIELDS):
        for pz in (0, 1):
            for px in (0, 1):
                t = 4 * field + 2 * pz + px
                for zc in (0, 1):
                    plane = 2 * zc + pz
                    if field < 3:
                        piece = cond_in[field, plane, pl.ds(px, 4, stride=2), :]
                    else:
                        source = mass_in if field == 3 else res_in
                        piece = source[plane, pl.ds(px, 4, stride=2), :]
                    own[t, pl.ds(zc, 4, stride=2), :] = piece
                halves = lanes_of(own[t], to_halves)
                own[t] = halves
                packed = lanes_of(halves, to_strip)
                word, group = divmod(t, 8)
                if packs[word] is None:
                    packs[word] = packed
                else:
                    packs[word] = jnp.where((lane >> 4) == group, packed, packs[word])
    for word in range(3):
        strip[word] = packs[word]

    pl.semaphore_wait(barrier, neighbours)

    def copy_to(n):
        sx, sy = DIRECTIONS[n]
        if sy == 0:
            source, target = own, side.at[0 if sx == 1 else 1]
        else:
            source, target = strip, strips.at[n]
        return pltpu.make_async_remote_copy(
            src_ref=source,
            dst_ref=target,
            send_sem=send_sem.at[n],
            recv_sem=recv_sem.at[n],
            device_id=(parts_at, gx + sx, gy + sy),
            device_id_type=MESH,
        )

    for n, (sx, sy) in enumerate(DIRECTIONS):
        @pl.when(present(sx, sy))
        def _():
            copy_to(n).start()

    own_copy = pltpu.make_async_copy(own, own_hbm, out_sem.at[0])
    own_copy.start()
    roots = field_roots(point_ref, gen_ref, zoff_ref, *place_of(counts, widths))
    for n, cls in enumerate(CLASSES):
        roots_out[n] = roots[cls]
    roots_copy = pltpu.make_async_copy(roots_out, roots_hbm, out_sem.at[1])
    roots_copy.start()

    for n, (sx, sy) in enumerate(DIRECTIONS):
        @pl.when(present(-sx, -sy))
        def _():
            copy_to(n).wait_recv()

        @pl.when(present(sx, sy))
        def _():
            copy_to(n).wait_send()
    own_copy.wait()
    roots_copy.wait()


def assemble(own, side, strips, wide):
    lane = lax.broadcasted_iota(jnp.int32, (8, LANES), 1)
    half = LANES // 2
    step = lane & 15
    merged = []
    for from_x in (-1, 0, 1):
        from_low = strips.at[DIRECTIONS.index((-from_x, 1))]
        from_high = strips.at[DIRECTIONS.index((-from_x, -1))]
        merged.append([jnp.where(step < 8, from_low[w], from_high[w]) for w in range(3)])
    for t in range(4 * FIELDS):
        word, group = divmod(t, 8)
        for block in range(3):
            tile = (side.at[0], own, side.at[1])[block][t]
            strip_tile = merged[block][word]
            for py in (0, 1):
                index = 16 * group + 4 * py + jnp.where(lane < half + 8, lane - half + 8, lane - (LANES - 4))
                index = jnp.where((lane >= half) & ((lane < half + 4) | (lane >= LANES - 4)), index, 0)
                edge = lanes_of(strip_tile, index)
                middle = pltpu.roll(tile, half, 1) if py else tile
                wide[2 * t + py, pl.ds(8 * block, 8), :] = jnp.where(lane < half, middle, edge)


def setup(
    counts, widths, own_hbm, side_hbm, strips_hbm, roots_hbm, stencil_hbm, solution_hbm,
    own, side, strips, roots_ref, wide, rows_out, stencil_out, solution_out, in_sem, sem,
):
    loads = [
        pltpu.make_async_copy(source, target, in_sem.at[n])
        for n, (source, target) in enumerate(
            ((own_hbm, own), (side_hbm, side), (strips_hbm, strips), (roots_hbm, roots_ref))
        )
    ]
    for load in loads:
        load.start()
    for load in loads:
        load.wait()
    assemble(own, side, strips, wide)

    def base(field, cls):
        return wide[8 * field + 4 * cls[0] + 2 * cls[1] + cls[2]]

    half = LANES // 2
    roots = {cls: roots_ref[n] for n, cls in enumerate(CLASSES)}
    cond, mass, residual = coefficients(base, roots, *place_of(counts, widths))
    stencil, rhs = galerkin(cond, mass, residual)
    for (dz, dx, dy), value in stencil.items():
        rows_out[9 * (dz + 1) + 3 * (dx + 1) + (dy + 1)] = value[8:16]
    for zc in (0, 1):
        for d in range(27):
            stencil_out[d, zc] = rows_out[d, pl.ds(zc, 4, stride=2), :][:, :half]
    stencil_copy = pltpu.make_async_copy(stencil_out, stencil_hbm, sem.at[0])
    stencil_copy.start()
    rows_out[27] = sweep_all(stencil, rhs)[8:16]
    for zc in (0, 1):
        solution_out[zc] = rows_out[27, pl.ds(zc, 4, stride=2), :][:, :half]
    solution_copy = pltpu.make_async_copy(solution_out, solution_hbm, sem.at[1])
    solution_copy.start()
    stencil_copy.wait()
    solution_copy.wait()


def solution(mesh):
    counts = (mesh.shape["gx"], mesh.shape["gy"])

    def on_device(base_cond, base_mass, fine_residual, point_index, gen_vector, z_offset):
        planes, width_x, width_y = base_mass.shape
        assert (planes, width_x, width_y) == (4, 8, LANES)
        tiles = 4 * FIELDS
        widths = (width_x, width_y)
        row_shape = (tiles, 8, LANES)
        moved = (row_shape, (2,) + row_shape, (8, 3, 8, LANES), (8, ROWS, LANES))
        whole = pl.BlockSpec(memory_space=pltpu.HBM)
        between = pl.pallas_call(
            functools.partial(exchange, counts, widths),
            out_shape=tuple(jax.ShapeDtypeStruct(shape, jnp.float32) for shape in moved),
            in_specs=[whole] * 6,
            out_specs=[whole] * 4,
            scratch_shapes=[
                pltpu.VMEM((3, planes, width_x, width_y), jnp.float32),
                pltpu.VMEM((planes, width_x, width_y), jnp.float32),
                pltpu.VMEM((planes, width_x, width_y), jnp.float32),
                pltpu.SMEM((1, 1), jnp.int32),
                pltpu.SMEM((MODES,), jnp.int32),
                pltpu.SMEM((1, 1), jnp.int32),
                pltpu.VMEM(row_shape, jnp.float32),
                pltpu.VMEM((3, 8, LANES), jnp.float32),
                pltpu.VMEM((8, ROWS, LANES), jnp.float32),
                pltpu.SemaphoreType.DMA((6,)),
                pltpu.SemaphoreType.DMA((8,)),
                pltpu.SemaphoreType.DMA((8,)),
                pltpu.SemaphoreType.DMA((2,)),
            ],
            compiler_params=pltpu.CompilerParams(
                collective_id=0, has_side_effects=True, vmem_limit_bytes=VMEM_GRANT
            ),
            name="exchange",
        )(
            base_cond, base_mass, fine_residual,
            point_index.reshape(1, 1), gen_vector, z_offset.reshape(1, 1),
        )
        out_planes, out_x, out_y = planes // 2, width_x // 2, width_y // 2
        stencil_shape, solution_shape = (27, out_planes, out_x, out_y), (out_planes, out_x, out_y)
        return pl.pallas_call(
            functools.partial(setup, counts, widths),
            out_shape=(
                jax.ShapeDtypeStruct(stencil_shape, jnp.float32),
                jax.ShapeDtypeStruct(solution_shape, jnp.float32),
            ),
            in_specs=[whole] * 4,
            out_specs=[whole] * 2,
            scratch_shapes=[pltpu.VMEM(shape, jnp.float32) for shape in moved]
            + [
                pltpu.VMEM((2 * tiles, ROWS, LANES), jnp.float32),
                pltpu.VMEM((28, 8, LANES), jnp.float32),
                pltpu.VMEM(stencil_shape, jnp.float32),
                pltpu.VMEM(solution_shape, jnp.float32),
                pltpu.SemaphoreType.DMA((4,)),
                pltpu.SemaphoreType.DMA((2,)),
            ],
            compiler_params=pltpu.CompilerParams(vmem_limit_bytes=VMEM_GRANT),
            name="setup",
        )(*between)

    return jax.shard_map(
        on_device,
        mesh=mesh,
        in_specs=(
            P(None, None, "gx", "gy"),
            P(None, "gx", "gy"),
            P("parts", "gx", "gy"),
            P("parts"),
            P(),
            P(),
        ),
        out_specs=(P(None, "parts", "gx", "gy"), P("parts", "gx", "gy")),
        check_vma=False,
    )
```

profile of v0, /device:TPU:0, one launch (start us, length us, event | category | flops | bytes accessed | tf_op | source)
XLA Modules:
  0.0 12.6 jit_solution(15035919484846551995)
XLA Ops:
  1.9 7.9 %exchange.1 = (f32[20,8,128]{2,1,0:T(8,128)}, f32[2,20,8,128]{3,2,1,0:T(8,128)}, f32[8,3,8,128]{3,2,1,0:T(8,128)}, f32[8,24,128]{2,1,0:T(8,128)}) custom-call(f32[3,4,8,128]{3,2,1,0:T(8,128)} %cond_hbm.1, f32[4,8,128]{2,1,0:T(8,128)} %mass_hbm.1, f32[4,8,128]{2,1,0:T(8,128)} %res_hbm.1, s32[1,1]{1,0:T(1,128)} %bitcast.2.point_hbm, s32[32]{0:T(128)} %gen_hbm.1, ...), custom_call_target="tpu_custom_call" | custom-call | tf_op jit(solution)/shard_map/exchange/pallas_call | solution.py:437
  9.9 2.7 %setup.1 = (f32[27,2,4,64]{3,2,1,0:T(4,128)}, f32[2,4,64]{2,1,0:T(4,128)}) custom-call(f32[20,8,128]{2,1,0:T(8,128)} %get-tuple-element.6.own_hbm, f32[2,20,8,128]{3,2,1,0:T(8,128)} %get-tuple-element.7.side_hbm, f32[8,3,8,128]{3,2,1,0:T(8,128)} %get-tuple-element.8.strips_hbm, f32[8,24,128]{2,1,0:T(8,128)} %get-tuple-element.9.roots_hbm), custom_call_target="tpu_custom_call" | custom-call | tf_op jit(solution)/shard_map/setup/pallas_call | solution.py:467
where the time goes:
time: 12.8 us; the launch traced here: 12.6 us
  Pallas kernels  10.7 us (84%)
  between operations  1.93 us (15%)
    pallas_call x1, Pallas kernels, on_device(): pl.pallas_call(functools.partial(exchange, counts, widths), out_shape=tup...  7.94 us
    pallas_call x1, Pallas kernels, on_device(): pl.pallas_call(functools.partial(setup, counts, widths), out_shape=(jax.S...  2.74 us

commit v1 on v0

--- a/solution.py
+++ b/solution.py
@@ -53,10 +53,17 @@
     return lanes_of(tile, index)
 
 
-def field_roots(point_ref, gen_ref, zoff_ref, x_first, y_first, nx_total, ny_total):
+def halves_of(value):
+    high = value.astype(jnp.bfloat16)
+    return high, (value - high.astype(jnp.float32)).astype(jnp.bfloat16)
+
+
+def field_roots(scalars, x_first, y_first, nx_total, ny_total):
+    half = MODES // 2
+    point_ref, gen_ref, zoff_ref = scalars
     point = point_ref[0, 0]
     lane = lax.broadcasted_iota(jnp.int32, (1, 2 * MODES), 1)
-    mode = jnp.where(lane < MODES, lane, lane - MODES)
+    mode = (lane & (half - 1)) + jnp.where(lane < MODES, 0, half)
     shifts = jnp.zeros((1, 2 * MODES), jnp.int32)
     for k in range(MODES):
         shifts = jnp.where(mode == k, (point * gen_ref[k]) & (QMCN - 1), shifts)
@@ -64,7 +71,7 @@
     amplitude = (shifts.astype(jnp.float32) / QMCN - 0.5) * (1.2 / (1.0 + 0.5 * modef))
     freq_z = modef - 5.0 * jnp.floor((modef + 0.5) * 0.2)
     freq_x = (1 + (mode & 3)).astype(jnp.float32)
-    phase = modef * (0.7 / (2.0 * math.pi)) - jnp.where(lane < MODES, 0.0, 0.25)
+    phase = modef * (0.7 / (2.0 * math.pi)) - jnp.where((lane & half) == 0, 0.0, 0.25)
     row = lax.broadcasted_iota(jnp.int32, (ROWS, 1), 0)
     z_row = (zoff_ref[0, 0] + 2 * (row & 1)).astype(jnp.float32) + 0.5
     x_row = (x_first + 2 * ((row >> 1) - HALO)).astype(jnp.float32) + 0.5
@@ -73,9 +80,10 @@
         turns = (z_row + pz) * (freq_z / (2.0 * NZG)) + (x_row + px) * (freq_x / (2.0 * nx_total))
         left.append(amplitude * cos_turns(turns + phase))
     left = jnp.concatenate(left, axis=0)
-    mode_row = lax.broadcasted_iota(jnp.int32, (2 * MODES, 1), 0)
+    left = left[:, :MODES] + left[:, MODES:]
+    mode_row = lax.broadcasted_iota(jnp.int32, (MODES, 1), 0)
     freq_y = (1 + ((mode_row >> 2) & 3)).astype(jnp.float32)
-    quarter = jnp.where(mode_row < MODES, 0.0, 0.25)
+    quarter = jnp.where(mode_row < half, 0.0, 0.25)
     place = lax.broadcasted_iota(jnp.int32, (1, LANES), 1)
     coarse = jnp.where(place < LANES // 2 + HALO, place, place - LANES)
     right = []
@@ -83,7 +91,13 @@
         y_place = (y_first + 2 * coarse + py).astype(jnp.float32) + 0.5
         right.append(cos_turns(freq_y * (y_place / (2.0 * ny_total)) + quarter))
     right = jnp.concatenate(right, axis=1)
-    logs = jnp.dot(left, right, precision=lax.Precision.HIGHEST, preferred_element_type=jnp.float32)
+    left_high, left_low = halves_of(left)
+    right_high, right_low = halves_of(right)
+    logs = jnp.dot(
+        jnp.concatenate([left_high, left_high, left_low], axis=1),
+        jnp.concatenate([right_high, right_low, right_high], axis=0),
+        preferred_element_type=jnp.float32,
+    )
     roots = jnp.exp(0.5 * logs)
     out = {}
     for n, (pz, px) in enumerate(itertools.product((0, 1), repeat=2)):
@@ -244,7 +258,7 @@
 def exchange(
     counts, widths, cond_hbm, mass_hbm, res_hbm, point_hbm, gen_hbm, zoff_hbm,
     own_hbm, side, strips, roots_hbm,
-    cond_in, mass_in, res_in, point_ref, gen_ref, zoff_ref, own, strip, roots_out,
+    cond_in, mass_in, res_in, point_ref, gen_ref, zoff_ref, own, low, high, roots_out,
     in_sem, send_sem, recv_sem, out_sem,
 ):
     parts_at = lax.axis_index("parts")
@@ -292,11 +306,10 @@
     lane = lax.broadcasted_iota(jnp.int32, (8, LANES), 1)
     half = LANES // 2
     to_halves = jnp.where(lane < half, 2 * lane, 2 * lane - (LANES - 1))
-    step = lane & 15
-    to_strip = step + jnp.where(
-        step < 4, half - 4, jnp.where(step < 8, LANES - 8, jnp.where(step < 12, -8, half - 12))
-    )
-    packs = [None] * 3
+    step = lane & 7
+    to_low = step + jnp.where(step < 4, half - 4, LANES - 8)
+    to_high = step + jnp.where(step < 4, 0, half - 4)
+    packs = [None] * 4
     for field in range(FIELDS):
         for pz in (0, 1):
             for px in (0, 1):
@@ -311,14 +324,16 @@
                     own[t, pl.ds(zc, 4, stride=2), :] = piece
                 halves = lanes_of(own[t], to_halves)
                 own[t] = halves
-                packed = lanes_of(halves, to_strip)
-                word, group = divmod(t, 8)
-                if packs[word] is None:
-                    packs[word] = packed
-                else:
-                    packs[word] = jnp.where((lane >> 4) == group, packed, packs[word])
-    for word in range(3):
-        strip[word] = packs[word]
+                word, place = divmod(t, 16)
+                for slot, packed in (
+                    (word, lanes_of(halves, to_low)),
+                    (2 + word, lanes_of(halves, to_high)),
+                ):
+                    if place:
+                        packed = jnp.where((lane >> 3) == place, packed, packs[slot])
+                    packs[slot] = packed
+    for word in (0, 1):
+        low[word], high[word] = packs[word], packs[2 + word]
 
     pl.semaphore_wait(barrier, neighbours)
 
@@ -327,7 +342,7 @@
         if sy == 0:
             source, target = own, side.at[0 if sx == 1 else 1]
         else:
-            source, target = strip, strips.at[n]
+            source, target = low if sy == 1 else high, strips.at[n]
         return pltpu.make_async_remote_copy(
             src_ref=source,
             dst_ref=target,
@@ -344,7 +359,7 @@
 
     own_copy = pltpu.make_async_copy(own, own_hbm, out_sem.at[0])
     own_copy.start()
-    roots = field_roots(point_ref, gen_ref, zoff_ref, *place_of(counts, widths))
+    roots = field_roots((point_ref, gen_ref, zoff_ref), *place_of(counts, widths))
     for n, cls in enumerate(CLASSES):
         roots_out[n] = roots[cls]
     roots_copy = pltpu.make_async_copy(roots_out, roots_hbm, out_sem.at[1])
@@ -365,17 +380,27 @@
 def assemble(own, side, strips, wide):
     lane = lax.broadcasted_iota(jnp.int32, (8, LANES), 1)
     half = LANES // 2
-    step = lane & 15
+    even = (lane & 8) == 0
     merged = []
     for from_x in (-1, 0, 1):
         from_low = strips.at[DIRECTIONS.index((-from_x, 1))]
         from_high = strips.at[DIRECTIONS.index((-from_x, -1))]
-        merged.append([jnp.where(step < 8, from_low[w], from_high[w]) for w in range(3)])
+        words = []
+        for word in (0, 1):
+            low, high = from_low[word], from_high[word]
+            words.append(
+                (
+                    jnp.where(even, low, pltpu.roll(high, 8, 1)),
+                    jnp.where(even, pltpu.roll(low, LANES - 8, 1), high),
+                )
+            )
+        merged.append(words)
     for t in range(4 * FIELDS):
-        word, group = divmod(t, 8)
+        word, place = divmod(t, 16)
+        group, odd = divmod(place, 2)
         for block in range(3):
             tile = (side.at[0], own, side.at[1])[block][t]
-            strip_tile = merged[block][word]
+            strip_tile = merged[block][word][odd]
             for py in (0, 1):
                 index = 16 * group + 4 * py + jnp.where(lane < half + 8, lane - half + 8, lane - (LANES - 4))
                 index = jnp.where((lane >= half) & ((lane < half + 4) | (lane >= LANES - 4)), index, 0)
@@ -432,7 +457,7 @@
         tiles = 4 * FIELDS
         widths = (width_x, width_y)
         row_shape = (tiles, 8, LANES)
-        moved = (row_shape, (2,) + row_shape, (8, 3, 8, LANES), (8, ROWS, LANES))
+        moved = (row_shape, (2,) + row_shape, (8, 2, 8, LANES), (8, ROWS, LANES))
         whole = pl.BlockSpec(memory_space=pltpu.HBM)
         between = pl.pallas_call(
             functools.partial(exchange, counts, widths),
@@ -447,7 +472,8 @@
                 pltpu.SMEM((MODES,), jnp.int32),
                 pltpu.SMEM((1, 1), jnp.int32),
                 pltpu.VMEM(row_shape, jnp.float32),
-                pltpu.VMEM((3, 8, LANES), jnp.float32),
+                pltpu.VMEM((2, 8, LANES), jnp.float32),
+                pltpu.VMEM((2, 8, LANES), jnp.float32),
                 pltpu.VMEM((8, ROWS, LANES), jnp.float32),
                 pltpu.SemaphoreType.DMA((6,)),
                 pltpu.SemaphoreType.DMA((8,)),

time: 12.8 us -> 12.8 us (level)
  no operation moved by 1% of the time
where the time goes in v1:
time: 12.8 us; the launch traced here: 12.6 us
  Pallas kernels  10.7 us (84%)
  between operations  1.93 us (15%)
    pallas_call x1, Pallas kernels, on_device(): pl.pallas_call(functools.partial(exchange, counts, widths), out_shape=tup...  7.93 us
    pallas_call x1, Pallas kernels, on_device(): pl.pallas_call(functools.partial(setup, counts, widths), out_shape=(jax.S...  2.75 us

profile of v1, /device:TPU:0, one launch (start us, length us, event | category | flops | bytes accessed | tf_op | source)
XLA Modules:
  0.0 12.6 jit_solution(12515015090720420410)
XLA Ops:
  1.9 7.9 %exchange.1 = (f32[20,8,128]{2,1,0:T(8,128)}, f32[2,20,8,128]{3,2,1,0:T(8,128)}, f32[8,2,8,128]{3,2,1,0:T(8,128)}, f32[8,24,128]{2,1,0:T(8,128)}) custom-call(f32[3,4,8,128]{3,2,1,0:T(8,128)} %cond_hbm.1, f32[4,8,128]{2,1,0:T(8,128)} %mass_hbm.1, f32[4,8,128]{2,1,0:T(8,128)} %res_hbm.1, s32[1,1]{1,0:T(1,128)} %bitcast.2.point_hbm, s32[32]{0:T(128)} %gen_hbm.1, ...), custom_call_target="tpu_custom_call" | custom-call | tf_op jit(solution)/shard_map/exchange/pallas_call | solution.py:462
  9.9 2.7 %setup.1 = (f32[27,2,4,64]{3,2,1,0:T(4,128)}, f32[2,4,64]{2,1,0:T(4,128)}) custom-call(f32[20,8,128]{2,1,0:T(8,128)} %get-tuple-element.6.own_hbm, f32[2,20,8,128]{3,2,1,0:T(8,128)} %get-tuple-element.7.side_hbm, f32[8,2,8,128]{3,2,1,0:T(8,128)} %get-tuple-element.8.strips_hbm, f32[8,24,128]{2,1,0:T(8,128)} %get-tuple-element.9.roots_hbm), custom_call_target="tpu_custom_call" | custom-call | tf_op jit(solution)/shard_map/setup/pallas_call | solution.py:493

commit v2 on v1

--- a/solution.py
+++ b/solution.py
@@ -19,7 +19,9 @@
 CLASSES = list(itertools.product((0, 1), repeat=3))
 FIELDS = 5
 AXIS_FIELD = (2, 0, 1)
-DIRECTIONS = [(sx, sy) for sx in (-1, 0, 1) for sy in (-1, 0, 1) if (sx, sy) != (0, 0)]
+DIRECTIONS = [(1, 0), (-1, 0), (0, 1), (0, -1), (1, 1), (1, -1), (-1, 1), (-1, -1)]
+CORNERS = DIRECTIONS[4:]
+STRIP = 60
 ROWS = 24
 LANES = 128
 VMEM_GRANT = 60 * 1024 * 1024
@@ -257,8 +259,8 @@
 
 def exchange(
     counts, widths, cond_hbm, mass_hbm, res_hbm, point_hbm, gen_hbm, zoff_hbm,
-    own_hbm, side, strips, roots_hbm,
-    cond_in, mass_in, res_in, point_ref, gen_ref, zoff_ref, own, low, high, roots_out,
+    wide_hbm, side, strips, roots_hbm,
+    cond_in, mass_in, res_in, point_ref, gen_ref, zoff_ref, own, strip, beside, wide, roots_out,
     in_sem, send_sem, recv_sem, out_sem,
 ):
     parts_at = lax.axis_index("parts")
@@ -306,10 +308,14 @@
     lane = lax.broadcasted_iota(jnp.int32, (8, LANES), 1)
     half = LANES // 2
     to_halves = jnp.where(lane < half, 2 * lane, 2 * lane - (LANES - 1))
-    step = lane & 7
-    to_low = step + jnp.where(step < 4, half - 4, LANES - 8)
-    to_high = step + jnp.where(step < 4, 0, half - 4)
-    packs = [None] * 4
+    first, last = lane & 7, (lane - STRIP) & 7
+    to_strip = jnp.where(
+        lane < STRIP,
+        first + jnp.where(first < 4, 0, half - 4),
+        last + jnp.where(last < 4, half - 4, LANES - 8),
+    )
+    slot = jnp.where(lane < STRIP, lane >> 3, (lane - STRIP) >> 3)
+    packs = [None] * 3
     for field in range(FIELDS):
         for pz in (0, 1):
             for px in (0, 1):
@@ -324,16 +330,11 @@
                     own[t, pl.ds(zc, 4, stride=2), :] = piece
                 halves = lanes_of(own[t], to_halves)
                 own[t] = halves
-                word, place = divmod(t, 16)
-                for slot, packed in (
-                    (word, lanes_of(halves, to_low)),
-                    (2 + word, lanes_of(halves, to_high)),
-                ):
-                    if place:
-                        packed = jnp.where((lane >> 3) == place, packed, packs[slot])
-                    packs[slot] = packed
-    for word in (0, 1):
-        low[word], high[word] = packs[word], packs[2 + word]
+                word, place = divmod(t, 7)
+                packed = lanes_of(halves, to_strip)
+                packs[word] = jnp.where(slot == place, packed, packs[word]) if place else packed
+    for word in range(3):
+        strip[word] = packs[word]
 
     pl.semaphore_wait(barrier, neighbours)
 
@@ -342,7 +343,8 @@
         if sy == 0:
             source, target = own, side.at[0 if sx == 1 else 1]
         else:
-            source, target = low if sy == 1 else high, strips.at[n]
+            source = strip
+            target = strips.at[n - 4] if sx else beside.at[0 if sy == 1 else 1]
         return pltpu.make_async_remote_copy(
             src_ref=source,
             dst_ref=target,
@@ -357,73 +359,68 @@
         def _():
             copy_to(n).start()
 
-    own_copy = pltpu.make_async_copy(own, own_hbm, out_sem.at[0])
-    own_copy.start()
     roots = field_roots((point_ref, gen_ref, zoff_ref), *place_of(counts, widths))
     for n, cls in enumerate(CLASSES):
         roots_out[n] = roots[cls]
     roots_copy = pltpu.make_async_copy(roots_out, roots_hbm, out_sem.at[1])
     roots_copy.start()
 
-    for n, (sx, sy) in enumerate(DIRECTIONS):
-        @pl.when(present(-sx, -sy))
-        def _():
-            copy_to(n).wait_recv()
-
-        @pl.when(present(sx, sy))
-        def _():
-            copy_to(n).wait_send()
-    own_copy.wait()
+    def finish(directions):
+        for direction in directions:
+            n = DIRECTIONS.index(direction)
+
+            @pl.when(present(-direction[0], -direction[1]))
+            def _():
+                copy_to(n).wait_recv()
+
+            @pl.when(present(*direction))
+            def _():
+                copy_to(n).wait_send()
+
+    finish(DIRECTIONS[2:4])
+    assemble(own, beside.at[0], beside.at[1], wide, 0)
+    wide_copy = pltpu.make_async_copy(wide, wide_hbm, out_sem.at[0])
+    wide_copy.start()
+    finish(DIRECTIONS[:2] + CORNERS)
     roots_copy.wait()
-
-
-def assemble(own, side, strips, wide):
+    wide_copy.wait()
+
+
+def assemble(tiles, from_low, from_high, wide, first_row):
     lane = lax.broadcasted_iota(jnp.int32, (8, LANES), 1)
     half = LANES // 2
-    even = (lane & 8) == 0
-    merged = []
-    for from_x in (-1, 0, 1):
-        from_low = strips.at[DIRECTIONS.index((-from_x, 1))]
-        from_high = strips.at[DIRECTIONS.index((-from_x, -1))]
-        words = []
-        for word in (0, 1):
-            low, high = from_low[word], from_high[word]
-            words.append(
-                (
-                    jnp.where(even, low, pltpu.roll(high, 8, 1)),
-                    jnp.where(even, pltpu.roll(low, LANES - 8, 1), high),
-                )
-            )
-        merged.append(words)
+    merged = [jnp.where(lane < STRIP, from_high[w], from_low[w]) for w in range(3)]
     for t in range(4 * FIELDS):
-        word, place = divmod(t, 16)
-        group, odd = divmod(place, 2)
-        for block in range(3):
-            tile = (side.at[0], own, side.at[1])[block][t]
-            strip_tile = merged[block][word][odd]
-            for py in (0, 1):
-                index = 16 * group + 4 * py + jnp.where(lane < half + 8, lane - half + 8, lane - (LANES - 4))
-                index = jnp.where((lane >= half) & ((lane < half + 4) | (lane >= LANES - 4)), index, 0)
-                edge = lanes_of(strip_tile, index)
-                middle = pltpu.roll(tile, half, 1) if py else tile
-                wide[2 * t + py, pl.ds(8 * block, 8), :] = jnp.where(lane < half, middle, edge)
+        tile = tiles[t]
+        word, place = divmod(t, 7)
+        for py in (0, 1):
+            edge = pltpu.roll(merged[word], half - 8 * place - 4 * py, 1)
+            middle = pltpu.roll(tile, half, 1) if py else tile
+            wide[2 * t + py, pl.ds(first_row, 8), :] = jnp.where(lane < half, middle, edge)
 
 
 def setup(
-    counts, widths, own_hbm, side_hbm, strips_hbm, roots_hbm, stencil_hbm, solution_hbm,
-    own, side, strips, roots_ref, wide, rows_out, stencil_out, solution_out, in_sem, sem,
+    counts, widths, wide_hbm, side_hbm, strips_hbm, roots_hbm, stencil_hbm, solution_hbm,
+    side, strips, roots_ref, wide, rows_out, stencil_out, solution_out, in_sem, sem,
 ):
     loads = [
         pltpu.make_async_copy(source, target, in_sem.at[n])
         for n, (source, target) in enumerate(
-            ((own_hbm, own), (side_hbm, side), (strips_hbm, strips), (roots_hbm, roots_ref))
+            (
+                (side_hbm, side),
+                (strips_hbm, strips),
+                (wide_hbm, wide.at[:, pl.ds(8, 8)]),
+                (roots_hbm, roots_ref),
+            )
         )
     ]
     for load in loads:
         load.start()
     for load in loads:
         load.wait()
-    assemble(own, side, strips, wide)
+    for block, sx in ((0, 1), (2, -1)):
+        from_low, from_high = (strips.at[CORNERS.index((sx, sy))] for sy in (1, -1))
+        assemble(side.at[block // 2], from_low, from_high, wide, 8 * block)
 
     def base(field, cls):
         return wide[8 * field + 4 * cls[0] + 2 * cls[1] + cls[2]]
@@ -457,7 +454,8 @@
         tiles = 4 * FIELDS
         widths = (width_x, width_y)
         row_shape = (tiles, 8, LANES)
-        moved = (row_shape, (2,) + row_shape, (8, 2, 8, LANES), (8, ROWS, LANES))
+        own_wide = (2 * tiles, 8, LANES)
+        moved = (own_wide, (2,) + row_shape, (4, 3, 8, LANES), (8, ROWS, LANES))
         whole = pl.BlockSpec(memory_space=pltpu.HBM)
         between = pl.pallas_call(
             functools.partial(exchange, counts, widths),
@@ -472,8 +470,9 @@
                 pltpu.SMEM((MODES,), jnp.int32),
                 pltpu.SMEM((1, 1), jnp.int32),
                 pltpu.VMEM(row_shape, jnp.float32),
-                pltpu.VMEM((2, 8, LANES), jnp.float32),
-                pltpu.VMEM((2, 8, LANES), jnp.float32),
+                pltpu.VMEM((3, 8, LANES), jnp.float32),
+                pltpu.VMEM((2, 3, 8, LANES), jnp.float32),
+                pltpu.VMEM(own_wide, jnp.float32),
                 pltpu.VMEM((8, ROWS, LANES), jnp.float32),
                 pltpu.SemaphoreType.DMA((6,)),
                 pltpu.SemaphoreType.DMA((8,)),
@@ -498,7 +497,7 @@
             ),
             in_specs=[whole] * 4,
             out_specs=[whole] * 2,
-            scratch_shapes=[pltpu.VMEM(shape, jnp.float32) for shape in moved]
+            scratch_shapes=[pltpu.VMEM(shape, jnp.float32) for shape in moved[1:]]
             + [
                 pltpu.VMEM((2 * tiles, ROWS, LANES), jnp.float32),
                 pltpu.VMEM((28, 8, LANES), jnp.float32),

time: 12.8 us -> 13.4 us (1.047)
  Pallas kernels: 10.7 us -> 11.3 us
    pallas_call x1, Pallas kernels: 7.93 us -> 8.67 us  [on_device(): pl.pallas_call(functools.partial(exchange, counts, widths), out_shape=tup...]
    pallas_call x1, Pallas kernels: 2.75 us -> 2.59 us  [on_device(): pl.pallas_call(functools.partial(setup, counts, widths), out_shape=(jax.S...]
where the time goes in v2:
time: 13.4 us; the launch traced here: 13.2 us
  Pallas kernels  11.3 us (84%)
  between operations  1.93 us (14%)
    pallas_call x1, Pallas kernels, on_device(): pl.pallas_call(functools.partial(exchange, counts, widths), out_shape=tup...  8.67 us
    pallas_call x1, Pallas kernels, on_device(): pl.pallas_call(functools.partial(setup, counts, widths), out_shape=(jax.S...  2.59 us

profile of v2, /device:TPU:0, one launch (start us, length us, event | category | flops | bytes accessed | tf_op | source)
XLA Modules:
  0.0 13.2 jit_solution(3863308497564778658)
XLA Ops:
  1.9 8.7 %exchange.1 = (f32[40,8,128]{2,1,0:T(8,128)}, f32[2,20,8,128]{3,2,1,0:T(8,128)}, f32[4,3,8,128]{3,2,1,0:T(8,128)}, f32[8,24,128]{2,1,0:T(8,128)}) custom-call(f32[3,4,8,128]{3,2,1,0:T(8,128)} %cond_hbm.1, f32[4,8,128]{2,1,0:T(8,128)} %mass_hbm.1, f32[4,8,128]{2,1,0:T(8,128)} %res_hbm.1, s32[1,1]{1,0:T(1,128)} %bitcast.2.point_hbm, s32[32]{0:T(128)} %gen_hbm.1, ...), custom_call_target="tpu_custom_call" | custom-call | tf_op jit(solution)/shard_map/exchange/pallas_call | solution.py:460
  10.6 2.6 %setup.1 = (f32[27,2,4,64]{3,2,1,0:T(4,128)}, f32[2,4,64]{2,1,0:T(4,128)}) custom-call(f32[40,8,128]{2,1,0:T(8,128)} %get-tuple-element.6.wide_hbm, f32[2,20,8,128]{3,2,1,0:T(8,128)} %get-tuple-element.7.side_hbm, f32[4,3,8,128]{3,2,1,0:T(8,128)} %get-tuple-element.8.strips_hbm, f32[8,24,128]{2,1,0:T(8,128)} %get-tuple-element.9.roots_hbm), custom_call_target="tpu_custom_call" | custom-call | tf_op jit(solution)/shard_map/setup/pallas_call | solution.py:492
